TPU v7x, 128 devices: a whole 4x4x4 slice. The times are simulated.
128 devices in a mesh: dp: 16 (over x, z_hi, core), tensor: 8 (over z_lo, y).
Axes of the slice: x: 4, y: 4, z: 4 (z_hi: 2, z_lo: 2; z = z_hi * 2 + z_lo), core: 2. Of those that a mesh axis runs over, the one named last changes fastest.
Arguments:
- acts: bfloat16 [2, 4096, 7168], P(None, 'dp'), may hold values from -6 to 6
- counts: int32 [16, 2], P('dp'), may hold values from 0 to 256, as said below
- gate_weight: bfloat16 [7168, 2048], P('dp', 'tensor'), may hold values from -0.0625 to 0.0625
- up_weight: bfloat16 [7168, 2048], P('dp', 'tensor'), may hold values from -0.0625 to 0.0625
- down_weight: bfloat16 [7168, 2048], P('dp', 'tensor'), may hold values from -0.125 to 0.125
- out_grad: bfloat16 [2, 4096, 7168], P(None, 'dp'), may hold values from -6 to 6
Outputs:
- mixed: bfloat16 [2, 4096, 7168], P(None, 'dp', 'tensor')
- input_grad: bfloat16 [2, 4096, 7168], P(None, 'dp', 'tensor')
- gate_grad: float32 [7168, 2048], P('dp', 'tensor')
- up_grad: float32 [7168, 2048], P('dp', 'tensor')
- down_grad: float32 [7168, 2048], P('dp', 'tensor')
Inputs may be any that keep to these rules, and one draw needn't show every extreme that they name: `counts`: every entry is a multiple of 128; the live rows of an index of dp in a micro-batch are its first slots; at least one entry equals 256.
All inputs are finite; a program needn't handle non-finite values.
Results may differ from a plain program's by a relative error of at most 0.02.
Values may be sent and summed in bfloat16 or wider, within the bound.
A program may use at most 128 MiB of HBM per device.

v0:
```python
import jax
import jax.numpy as jnp
from jax import lax
from jax.sharding import PartitionSpec as P


def contract_last(left, right):
    return lax.dot_general(
        left, right, (((1,), (1,)), ((), ())), preferred_element_type=jnp.float32
    )


def contract_first(left, right):
    return lax.dot_general(
        left, right, (((0,), (0,)), ((), ())), preferred_element_type=jnp.float32
    )


def local(acts, counts, gate_weight, up_weight, down_weight, out_grad):
    micro_count, row_count, model_width = acts.shape
    slice_width = gate_weight.shape[1]
    whole_gate, whole_up, whole_down = (
        lax.all_gather(gate_weight, "dp", axis=0, tiled=True),
        lax.all_gather(up_weight, "dp", axis=0, tiled=True),
        lax.all_gather(down_weight, "dp", axis=0, tiled=True),
    )
    position = lax.broadcasted_iota(jnp.int32, (micro_count, row_count), 1)
    live_rows = (position < counts[0][:, None]).astype(jnp.float32).reshape(-1, 1)
    flat_acts = acts.reshape(-1, model_width)
    flat_grad = out_grad.reshape(-1, model_width)
    gate_pre = jnp.dot(flat_acts, whole_gate, preferred_element_type=jnp.float32)
    up_pre = jnp.dot(flat_acts, whole_up, preferred_element_type=jnp.float32)
    sigma = jax.nn.sigmoid(gate_pre)
    activated = gate_pre * sigma
    hidden = (live_rows * activated * up_pre).astype(jnp.bfloat16)
    pieces = []
    for micro_index in range(micro_count):
        piece_rows = hidden[micro_index * row_count : (micro_index + 1) * row_count]
        pieces.append(
            lax.psum_scatter(
                contract_last(piece_rows, whole_down).astype(jnp.bfloat16),
                "tensor",
                scatter_dimension=1,
                tiled=True,
            ).astype(jnp.float32)
        )
    mixed = jnp.stack(pieces)
    grad_hidden = jnp.dot(flat_grad, whole_down, preferred_element_type=jnp.float32)
    slope = sigma * (1.0 + gate_pre * (1.0 - sigma))
    grad_gate_pre = (live_rows * grad_hidden * up_pre * slope).astype(jnp.bfloat16)
    grad_up_pre = (live_rows * grad_hidden * activated).astype(jnp.bfloat16)
    input_term = contract_last(grad_gate_pre, whole_gate) + contract_last(grad_up_pre, whole_up)
    input_grad = lax.psum_scatter(
        input_term.reshape(micro_count, row_count, model_width).astype(jnp.bfloat16),
        "tensor",
        scatter_dimension=2,
        tiled=True,
    )
    grad_columns = jnp.concatenate([grad_gate_pre, grad_up_pre], axis=1)
    totals = jnp.concatenate(
        [contract_first(flat_acts, grad_columns), contract_first(flat_grad, hidden)], axis=1
    )
    reduced = lax.psum_scatter(
        totals.astype(jnp.bfloat16), "dp", scatter_dimension=0, tiled=True
    ).astype(jnp.float32)
    gate_grad = reduced[:, :slice_width]
    up_grad = reduced[:, slice_width : 2 * slice_width]
    down_grad = reduced[:, 2 * slice_width :]
    return (mixed.astype(jnp.bfloat16), input_grad, gate_grad, up_grad, down_grad)


def solution(mesh):
    placed = (
        P(None, "dp", None),
        P("dp", None),
        P("dp", "tensor"),
        P("dp", "tensor"),
        P("dp", "tensor"),
        P(None, "dp", None),
    )
    return jax.shard_map(
        local,
        mesh=mesh,
        in_specs=placed,
        out_specs=(
            P(None, "dp", "tensor"),
            P(None, "dp", "tensor"),
            P("dp", "tensor"),
            P("dp", "tensor"),
            P("dp", "tensor"),
        ),
        check_vma=False,
    )
```

profile of v0, /device:TPU:34, one launch (start us, length us, event | category | flops | bytes accessed | tf_op | source)
XLA Modules:
  0.0 503.0 jit_solution(11541078492665922553)
XLA Ops:
  7.2 0.0 all-gather.4.cloned.1.call-start
  7.2 0.7 all-gather.4.cloned.1.call-update
  7.9 0.0 all-gather.6.cloned.1.call-start
  7.9 0.7 all-gather.6.cloned.1.call-update
  8.6 0.0 all-gather.8.cloned.1.call-start
  8.7 0.7 all-gather.8.cloned.1.call-update
  9.4 0.0 reduce-scatter.15.cloned.1.call-start
  9.4 0.7 fusion.8
  10.2 55.3 %all-gather.4.cloned.1.call-done = bf16[7168,256]{1,0:T(8,128)(2,1)} async-done(((bf16[448,256]{1,0:T(8,128)(2,1)}), bf16[7168,256]{1,0:T(8,128)(2,1)}) %all-gather.4.cloned.1.call-update) | async-done | bytes 3670032 | tf_op jit(solution)/shard_map/all_gather | solution.py:23
  65.4 6.2 %fusion.11 = f32[512,256]{0,1:T(8,128)S(1)} fusion(bf16[512,7168]{1,0:T(8,128)(2,1)} %bitcast.51, bf16[7168,256]{1,0:T(8,128)(2,1)} %all-gather.4.cloned.1.call-done), kind=kOutput, calls=%fused_computation.24 | convolution fusion | flops 1879048192 | bytes 11534336 | tf_op jit(solution)/shard_map/dot_general | solution.py:31
  71.7 49.0 %all-gather.6.cloned.1.call-done = bf16[7168,256]{1,0:T(8,128)(2,1)} async-done(((bf16[448,256]{1,0:T(8,128)(2,1)}), bf16[7168,256]{1,0:T(8,128)(2,1)}) %all-gather.6.cloned.1.call-update) | async-done | bytes 3670032 | tf_op jit(solution)/shard_map/all_gather | solution.py:24
  120.6 6.2 %fusion.12 = f32[512,256]{0,1:T(8,128)S(1)} fusion(bf16[512,7168]{1,0:T(8,128)(2,1)} %bitcast.52, bf16[7168,256]{1,0:T(8,128)(2,1)} %all-gather.6.cloned.1.call-done), kind=kOutput, calls=%fused_computation.25 | convolution fusion | flops 1879048192 | bytes 11534336 | tf_op jit(solution)/shard_map/dot_general | solution.py:32
  126.9 49.0 %all-gather.8.cloned.1.call-done = bf16[7168,256]{1,0:T(8,128)(2,1)} async-done(((bf16[448,256]{1,0:T(8,128)(2,1)}), bf16[7168,256]{1,0:T(8,128)(2,1)}) %all-gather.8.cloned.1.call-update) | async-done | bytes 3670032 | tf_op jit(solution)/shard_map/all_gather | solution.py:25
  175.9 0.0 copy-start
  175.9 6.6 %multiply_convert_fusion = (bf16[512,256]{0,1:T(8,128)(2,1)S(1)}, bf16[512,256]{0,1:T(8,128)(2,1)S(1)}, bf16[512,256]{0,1:T(8,128)(2,1)S(1)}) fusion(f32[512,256]{0,1:T(8,128)S(1)} %fusion.11, f32[512,256]{0,1:T(8,128)S(1)} %fusion.12, f32[512]{0:T(512)S(1)} %bitcast.47, bf16[512,7168]{1,0:T(8,128)(2,1)} %bitcast.49, ...), kind=kOutput, calls=%fused_computation.13 | convolution fusion | flops 1881276416 | bytes 12847104 | tf_op jit(solution)/shard_map/dot_general | solution.py:48
  182.4 0.0 copy-done
  182.4 3.0 convolution_convert_fusion.2
  185.4 5.9 %copy.19 = bf16[256,7168]{0,1:T(8,128)(2,1)} copy(bf16[256,7168]{1,0:T(8,128)(2,1)} %convolution_convert_fusion.2) | data formatting | bytes 7340032
  191.3 0.0 reduce-scatter.15.cloned.1.call-update
  191.4 0.0 reduce-scatter.13.cloned.1.call-start
  191.4 5.0 convolution_convert_fusion.3
  196.4 6.0 %copy.17 = bf16[256,7168]{0,1:T(8,128)(2,1)} copy(bf16[256,7168]{1,0:T(8,128)(2,1)} %convolution_convert_fusion.3) | data formatting | bytes 7340032
  202.4 0.0 reduce-scatter.13.cloned.1.call-update
  202.4 0.2 reduce-scatter.17.cloned.1.call-start
  202.7 0.0 copy-start.1
  202.7 9.5 %fusion.13 = f32[512,7168]{1,0:T(8,128)} fusion(bf16[512,256]{0,1:T(8,128)(2,1)S(1)} %get-tuple-element.16, bf16[7168,256]{1,0:T(8,128)(2,1)} %all-gather.4.cloned.1.call-done), kind=kOutput, calls=%fused_computation.26 | convolution fusion | flops 1879048192 | bytes 18612224 | tf_op jit(solution)/shard_map/dot_general | solution.py:8
  212.2 0.0 copy-done.1
  212.2 10.5 %add_convert_fusion = bf16[512,7168]{1,0:T(8,128)(2,1)} fusion(f32[512,7168]{1,0:T(8,128)} %fusion.13, bf16[512,256]{0,1:T(8,128)(2,1)S(1)} %get-tuple-element.15, bf16[7168,256]{1,0:T(8,128)(2,1)S(1)} %copy-done.1), kind=kOutput, calls=%fused_computation | convolution fusion | flops 1886388224 | bytes 25952256 | tf_op jit(solution)/shard_map/dot_general | solution.py:8
  222.7 18.6 %copy.21 = bf16[2,256,7168]{1,0,2:T(2,128)(2,1)} copy(bf16[2,256,7168]{2,1,0:T(8,128)(2,1)} %bitcast.39) | data formatting | bytes 14680064
  241.3 7.3 %copy.26 = bf16[896,8,2,256]{3,1,2,0:T(8,128)(2,1)} copy(bf16[896,8,2,256]{3,2,1,0:T(2,128)(2,1)} %bitcast.38) | data formatting | bytes 14680064
  248.6 0.0 reduce-scatter.17.cloned.1.call-update
  248.6 0.3 reduce-scatter.19.cloned.1.call-start
  248.9 5.5 %fusion.1 = bf16[7168,256]{0,1:T(8,128)(2,1)S(1)} fusion(bf16[512,256]{0,1:T(8,128)(2,1)S(1)} %get-tuple-element.17, bf16[512,7168]{1,0:T(8,128)(2,1)} %bitcast.50), kind=kOutput, calls=%fused_computation.7 | convolution fusion | flops 1880883200 | bytes 11272192 | tf_op jit(solution)/shard_map/dot_general | solution.py:14
  254.4 7.7 %fusion = bf16[7168,512]{0,1:T(8,128)(2,1)S(1)} fusion(bf16[512,7168]{1,0:T(8,128)(2,1)} %bitcast.53, bf16[512,256]{0,1:T(8,128)(2,1)S(1)} %get-tuple-element.15, bf16[512,256]{0,1:T(8,128)(2,1)S(1)} %get-tuple-element.16), kind=kOutput, calls=%fused_computation.3 | convolution fusion | flops 3762814976 | bytes 15204352 | tf_op jit(solution)/shard_map/dot_general | solution.py:14
  262.1 7.9 %pad_maximum_fusion = bf16[7168,768]{0,1:T(8,128)(2,1)} fusion(bf16[7168,256]{0,1:T(8,128)(2,1)S(1)} %fusion.1, bf16[7168,512]{0,1:T(8,128)(2,1)S(1)} %fusion), kind=kLoop, calls=%fused_computation.1 | loop fusion | flops 22020096 | bytes 22020096 | tf_op jit(solution)/shard_map/concatenate | solution.py:60
  270.0 14.8 %copy.23 = bf16[7168,768]{1,0:T(8,128)(2,1)} copy(bf16[7168,768]{0,1:T(8,128)(2,1)} %pad_maximum_fusion) | data formatting | bytes 22020096
  284.8 0.0 reduce-scatter.19.cloned.1.call-update
  284.8 0.0 reduce-scatter.15.cloned.1.call-done
  284.9 1.3 copy.20
  286.1 3.8 reduce-scatter.13.cloned.1.call-done
  289.9 1.3 copy.18
  291.2 1.0 pad_maximum_fusion.1
  292.2 81.9 %reduce-scatter.17.cloned.1.call-done = bf16[896,512]{1,0:T(8,128)(2,1)} async-done(((bf16[7168,512]{1,0:T(8,128)(2,1)}), bf16[896,512]{1,0:T(8,128)(2,1)}) %reduce-scatter.17.cloned.1.call-update) | async-done | bytes 917520
  374.1 2.4 reshape.45
  376.5 2.6 copy.22
  379.1 112.6 %reduce-scatter.19.cloned.1.call-done = bf16[448,768]{1,0:T(8,128)(2,1)} async-done(((bf16[7168,768]{1,0:T(8,128)(2,1)}), bf16[448,768]{1,0:T(8,128)(2,1)}) %reduce-scatter.19.cloned.1.call-update) | async-done | bytes 688144
  491.7 1.4 copy.24
  493.1 0.2 fusion.10
  493.3 1.0 copy.14
  494.3 1.0 copy.15
  495.2 1.0 copy.16
  (1 shorter events, 0.0 us)
Async XLA Ops:
  7.2 58.3 %all-gather.4.cloned.1.call-start = ((), (), s32[]{:S(2)}) async-start(), calls=%async_computation.4 | async-start | bytes 3899392 | tf_op jit(solution)/shard_map/all_gather | solution.py:23
  7.9 112.7 %all-gather.6.cloned.1.call-start = ((), (), s32[]{:S(2)}) async-start(), calls=%async_computation.5 | async-start | bytes 3899392 | tf_op jit(solution)/shard_map/all_gather | solution.py:24
  8.6 167.2 %all-gather.8.cloned.1.call-start = ((), (), s32[]{:S(2)}) async-start(), calls=%async_computation.6 | async-start | bytes 3899392 | tf_op jit(solution)/shard_map/all_gather | solution.py:25
  9.4 275.5 %reduce-scatter.15.cloned.1.call-start = ((), (), s32[]{:S(2)}) async-start(), calls=%async_computation.8 | async-start | bytes 4128768
  175.9 6.6 %copy-start = (bf16[7168,256]{1,0:T(8,128)(2,1)S(1)}, bf16[7168,256]{1,0:T(8,128)(2,1)}, u32[]{:S(2)}) copy-start(bf16[7168,256]{1,0:T(8,128)(2,1)} %all-gather.8.cloned.1.call-done) | copy-start | bytes 11010052
  191.4 98.6 %reduce-scatter.13.cloned.1.call-start = ((), (), s32[]{:S(2)}) async-start(), calls=%async_computation.7 | async-start | bytes 4128768
  202.4 171.7 %reduce-scatter.17.cloned.1.call-start = ((), (), s32[]{:S(2)}) async-start(), calls=%async_computation.9 | async-start | bytes 8257536
  202.7 9.5 %copy-start.1 = (bf16[7168,256]{1,0:T(8,128)(2,1)S(1)}, bf16[7168,256]{1,0:T(8,128)(2,1)}, u32[]{:S(2)}) copy-start(bf16[7168,256]{1,0:T(8,128)(2,1)} %all-gather.6.cloned.1.call-done) | copy-start | bytes 11010052
  248.6 243.1 %reduce-scatter.19.cloned.1.call-start = ((), (), s32[]{:S(2)}) async-start(), calls=%async_computation.10 | async-start | bytes 11698176
Sparse Core Ops, SparseCore 0:
  10.4 54.9 all-gather.3
  67.8 52.7 all-gather.5
  123.1 52.7 all-gather.7
  191.5 47.9 reduce-scatter.14
  241.7 48.1 reduce-scatter.12
  292.2 81.8 reduce-scatter.16
  378.5 113.1 reduce-scatter.18
where the time goes:
time: 506 us; the launch traced here: 503 us
  waiting for transfers between devices  354 us (70%)
  local copies, waits for them, and re-layouts  64.5 us (13%)
  matrix products  60.2 us (12%)
  between operations  14.2 us (3%)
  other arithmetic  9.65 us (2%)
    unnamed x11, waiting for transfers between devices  200 us
    unnamed x18, local copies, waits for them, and re-layouts  64.3 us
    all_gather x1, waiting for transfers between devices, local(): lax.all_gather(gate_weight, 'dp', axis=0, tiled=True)  55.3 us
    all_gather x1, waiting for transfers between devices, local(): lax.all_gather(down_weight, 'dp', axis=0, tiled=True)  49 us
    all_gather x1, waiting for transfers between devices, local(): lax.all_gather(up_weight, 'dp', axis=0, tiled=True)  49 us
    dot_general x4, matrix products, contract_last(): lax.dot_general(left, right, (((1,), (1,)), ((), ())), preferred_element_...  28 us
    dot_general x2, matrix products, contract_first(): lax.dot_general(left, right, (((0,), (0,)), ((), ())), preferred_element_...  13.2 us
  transfers between devices with their start and end apart: 7, of which 6 were waited for; matrix products, arithmetic and copies ran while one was open for 23% of the time, Pallas kernels for 0%

commit v1 on v0

v1 whole, which is shorter than its diff:
```python
import jax
import jax.numpy as jnp
from jax import lax
from jax.experimental import pallas as pl
from jax.experimental.pallas import tpu as pltpu
from jax.sharding import PartitionSpec as P

MESH = pl.DeviceIdType.MESH
GATE, UP, DOWN = 0, 1, 2
HIDDEN, GGP, GUP = 0, 1, 2
SHARD = 448
CHIP = 2 * SHARD
HALF = SHARD // 2
WIDTH = 256
ROWS = 512
MICRO_ROWS = 256


def aligned(index, size, unit):
    return pl.ds(pl.multiple_of(index * unit, unit), size)


def contract_last(left, right):
    return lax.dot_general(left, right, (((1,), (1,)), ((), ())), preferred_element_type=jnp.float32)


def contract_first(left, right):
    return lax.dot_general(left, right, (((0,), (0,)), ((), ())), preferred_element_type=jnp.float32)


def kernel(
    acts, counts, gate_w, up_w, down_w, out_grad,
    mixed, input_grad, gate_grad, up_grad, down_grad,
    av, ov, wf, w2, af, rs, rx, rz, pre, fin, res,
    load_sem, own_sem, a_send, a_recv, t_send, t_recv, u_send, u_recv,
    g_send, g_recv, b_send, b_recv, out_sem,
):
    dp, t = lax.axis_index("dp"), lax.axis_index("tensor")
    x, zh, c = dp // 4, (dp // 2) % 2, dp % 2
    zl, y = t // 4, t % 4
    weights = (gate_w, up_w, down_w)

    def device(dx=0, flip_zh=0, flip_c=0, flip_zl=0, dy=0):
        return (
            ((x + dx) % 4) * 4 + ((zh + flip_zh) % 2) * 2 + (c + flip_c) % 2,
            ((zl + flip_zl) % 2) * 4 + (y + dy) % 4,
        )

    def chip_of(r):
        return ((x + r % 4) % 4) * 2 + (zh + r // 4) % 2

    def remote(src, dst, send, recv, to):
        return pltpu.make_async_remote_copy(src, dst, send, recv, device_id=to, device_id_type=MESH)

    sibling = device(flip_c=1)
    across = device(flip_zh=1)
    my_cols = aligned(t, WIDTH, WIDTH)

    barrier = pltpu.get_barrier_semaphore()
    partners = [sibling, across] + [device(dx=j) for j in (1, 2, 3)]
    partners += [device(dy=j) for j in (1, 2, 3)]
    partners += [device(flip_zl=1, dy=j) for j in range(4)]
    partners += [device(flip_zl=1, flip_zh=1, dy=j) for j in range(4)]
    for to in partners:
        pl.semaphore_signal(barrier, inc=1, device_id=to, device_id_type=MESH)

    own = [pltpu.make_async_copy(weights[w], wf.at[w, aligned(dp, SHARD, SHARD)], own_sem.at[w]) for w in range(3)]
    for copy in own:
        copy.start()
    loads = []
    for which, (src, dst) in enumerate(((acts, av), (out_grad, ov))):
        for m in range(2):
            loads.append(
                pltpu.make_async_copy(
                    src.at[m], dst.at[pl.ds(m * MICRO_ROWS, MICRO_ROWS)], load_sem.at[2 * which + m]
                )
            )
    for copy in loads:
        copy.start()
    pl.semaphore_wait(barrier, len(partners))

    sends = {w: [] for w in range(3)}

    def shard_ref(w, r, core):
        return wf.at[w, aligned(chip_of(r) * 2 + core, SHARD, SHARD)]

    def move(w, r, to, send_index, recv_index, core=None):
        ref = shard_ref(w, r, c if core is None else core)
        copy = remote(ref, ref, a_send.at[w, send_index], a_recv.at[w, recv_index], to)
        copy.start()
        sends[w].append(copy)

    def wait_shard(w, r, core, index):
        ref = shard_ref(w, r, core)
        remote(ref, ref, a_send.at[w, index], a_recv.at[w, index], sibling).wait_recv()

    def transpose_parts(w, r, act):
        d = chip_of(r)
        to_zl, to_y = d // 4, d % 4
        cross = (to_zl + zl) % 2
        for h in range(2):
            src = wf.at[w, pl.ds(pl.multiple_of((d * 2 + c) * SHARD + h * HALF, HALF), HALF)]
            dst = w2.at[w, pl.ds(pl.multiple_of(c * SHARD + h * HALF, HALF), HALF), my_cols]
            to = (x * 4 + ((zh + h * cross) % 2) * 2 + c, d)

            @pl.when(d != t)
            def _():
                act[0](remote(src, dst, t_send.at[w, r, h], t_recv.at[w, t, h], to))

            @pl.when(d == t)
            def _():
                act[1](pltpu.make_async_copy(src, dst, t_send.at[w, r, h]))

    def start(copy):
        copy.start()

    def transpose_out(w, r):
        transpose_parts(w, r, (start, start))

    def pass_on(w, r):
        move(w, r, sibling, 8 + r, 8 + r)
        transpose_out(w, r)

    def send_own(w):
        own[w].wait()
        move(w, 0, across, 4, 4)
        for j in (1, 3, 2):
            move(w, 0, device(dx=j), j, 4 - j)
        pass_on(w, 0)

    def from_across(w):
        wait_shard(w, 4, c, 4)
        for j in (1, 3, 2):
            move(w, 4, device(dx=j), 4 + j, 8 - j)
        pass_on(w, 4)

    def from_x(w, base):
        for k in (1, 3, 2):
            wait_shard(w, base + k, c, base + k)
            pass_on(w, base + k)

    def from_sibling(w, relations):
        for r in relations:
            wait_shard(w, r, 1 - c, 8 + r)

    def accumulate(which, values, relations, step, first=False):
        @pl.loop(0, len(relations))
        def _(i):
            d = chip_of(relations[0] + i * step)
            cols = aligned(d, CHIP, CHIP)
            left = values[:, cols]
            for w in which:
                part = jnp.dot(left, wf[w, cols], preferred_element_type=jnp.float32)
                if first:
                    @pl.when(i == 0)
                    def _():
                        pre[w] = part

                    @pl.when(i > 0)
                    def _():
                        pre[w] += part
                else:
                    pre[w] += part

    def live_rows(i, size):
        per = MICRO_ROWS // size
        row = lax.broadcasted_iota(jnp.int32, (size, WIDTH), 0) + (i % per) * size
        return (row < counts[0, i // per]).astype(jnp.float32)

    TILE = 64

    def gather_out(a):
        block = af.at[a, :, my_cols]
        out = [remote(block, block, g_send.at[a, 0], g_recv.at[a, 0], device(flip_zl=1))]
        for j in (1, 3, 2):
            out.append(remote(block, block, g_send.at[a, j], g_recv.at[a, 4 - j], device(dy=j)))
        for copy in out:
            copy.start()
        return out

    def group(flip_zl, k):
        return aligned(((zl + flip_zl) % 2) * 4 + (y + k) % 4, WIDTH, WIDTH)

    def gather_forward(a):
        out = []
        block = af.at[a, :, group(1, 0)]
        remote(block, block, g_send.at[a, 0], g_recv.at[a, 0], sibling).wait_recv()
        part = af.at[a, pl.ds(MICRO_ROWS, MICRO_ROWS), group(1, 0)]
        for j in (1, 3, 2):
            copy = remote(part, part, g_send.at[a, 6 + j], g_recv.at[a, 10 - j], device(dy=j))
            copy.start()
            out.append(copy)
        for k in (1, 3, 2):
            block = af.at[a, :, group(0, k)]
            remote(block, block, g_send.at[a, k], g_recv.at[a, k], sibling).wait_recv()
            part = af.at[a, pl.ds(0, MICRO_ROWS), group(0, k)]
            copy = remote(part, part, g_send.at[a, 3 + k], g_recv.at[a, 3 + k], device(flip_zl=1))
            copy.start()
            out.append(copy)
        return out

    def gather_done(a):
        for k in (1, 3, 2):
            first = af.at[a, pl.ds(0, MICRO_ROWS), group(1, k)]
            remote(first, first, g_send.at[a, 3 + k], g_recv.at[a, 3 + k], sibling).wait_recv()
            second = af.at[a, pl.ds(MICRO_ROWS, MICRO_ROWS), group(1, k)]
            remote(second, second, g_send.at[a, 6 + k], g_recv.at[a, 6 + k], sibling).wait_recv()

    def finish_weight_sends(w):
        for copy in sends[w]:
            copy.wait_send()
        for r in range(8):
            transpose_parts(w, r, (lambda copy: copy.wait_send(), lambda copy: copy.wait()))

    def columns_arrived(w):
        for f in range(8):
            for h in range(2):
                dst = w2.at[
                    w, pl.ds(pl.multiple_of(c * SHARD + h * HALF, HALF), HALF), pl.ds(f * WIDTH, WIDTH)
                ]

                @pl.when(t != f)
                def _():
                    remote(dst, dst, t_send.at[w, f, h], t_recv.at[w, f, h], sibling).wait_recv()

        mine = w2.at[w, aligned(c, SHARD, SHARD)]
        copy = remote(mine, mine, u_send.at[w], u_recv.at[w], sibling)
        copy.start()
        return copy

    def columns_done(w):
        theirs = w2.at[w, aligned(1 - c, SHARD, SHARD)]
        remote(theirs, theirs, u_send.at[w], u_recv.at[w], sibling).wait_recv()

    place = {DOWN: GATE, GATE: UP, UP: DOWN}

    def dest(i):
        return ((x + 1 + i // 2) % 4) * 2 + i % 2

    def block_of(p, i, core):
        return wf.at[place[p], aligned(dest(i) * 2 + core, SHARD, SHARD)]

    def pair_copy(p, i):
        return remote(block_of(p, i, 1 - c), rs.at[p, i], b_send.at[p, i], b_recv.at[p, i], sibling)

    def grad_partials(p, values, a):
        @pl.loop(0, 8)
        def _(i):
            d = dest(i)
            part = contract_first(values[:, aligned(d, CHIP, CHIP)], af[a, :, my_cols])
            wf[place[p], aligned(d, CHIP, CHIP)] = part.astype(jnp.bfloat16)
            pair_copy(p, i).start()

    def x_copy(p, i):
        j, half = i // 2 + 1, i % 2
        slot = (3 - j) * 2 + half
        return remote(
            block_of(p, i, c), rx.at[p, slot], b_send.at[p, 8 + i], b_recv.at[p, 8 + slot], device(dx=j)
        )

    STEP = 112

    def pair_sums(p):
        q = place[p]
        for i in range(6):
            pair_copy(p, i).wait_recv()
            base = (dest(i) * 2 + c) * SHARD

            @pl.loop(0, SHARD // STEP)
            def _(s):
                rows = pl.ds(pl.multiple_of(base + s * STEP, 16), STEP)
                total = wf[q, rows].astype(jnp.float32) + rs[p, i, aligned(s, STEP, STEP)].astype(jnp.float32)
                wf[q, rows] = total.astype(jnp.bfloat16)

            x_copy(p, i).start()

    def z_copy(p):
        src = wf.at[place[p], aligned((x * 2 + 1 - zh) * 2 + c, SHARD, SHARD)]
        return remote(src, rz.at[p], b_send.at[p, 14], b_recv.at[p, 14], across)

    def x_sums(p):
        q = place[p]
        for i in (6, 7):
            pair_copy(p, i).wait_recv()
        for slot in range(6):
            remote(
                rx.at[p, slot], rx.at[p, slot], b_send.at[p, 8 + slot], b_recv.at[p, 8 + slot], sibling
            ).wait_recv()

        def total(half, s):
            rows = pl.ds(pl.multiple_of(((x * 2 + half) * 2 + c) * SHARD + s * STEP, 16), STEP)
            inner = aligned(s, STEP, STEP)
            value = wf[q, rows].astype(jnp.float32) + rs[p, 6 + half, inner].astype(jnp.float32)
            for k in range(3):
                value += rx[p, 2 * k + half, inner].astype(jnp.float32)
            return rows, value

        @pl.loop(0, SHARD // STEP)
        def _(s):
            rows, value = total(1 - zh, s)
            wf[q, rows] = value.astype(jnp.bfloat16)

        z_copy(p).start()

        @pl.loop(0, SHARD // STEP)
        def _(s):
            rows, value = total(zh, s)
            fin[p, aligned(s, STEP, STEP)] = value

    grads = {GATE: gate_grad, UP: up_grad, DOWN: down_grad}

    def z_sums(p):
        z_copy(p).wait_recv()

        @pl.loop(0, SHARD // STEP)
        def _(s):
            inner = aligned(s, STEP, STEP)
            fin[p, inner] += rz[p, inner].astype(jnp.float32)

        copy = pltpu.make_async_copy(fin.at[p], grads[p], out_sem.at[p])
        copy.start()
        return copy

    def write_out(ref, which):
        copies = []
        for m in range(2):
            copy = pltpu.make_async_copy(
                res.at[which, pl.ds(m * MICRO_ROWS, MICRO_ROWS)], ref.at[m], out_sem.at[3 + 2 * which + m]
            )
            copy.start()
            copies.append(copy)
        return copies

    OUT_TILE = 128

    send_own(GATE)
    send_own(UP)
    from_across(GATE)
    from_across(UP)
    send_own(DOWN)
    from_x(GATE, 0)
    from_x(UP, 0)
    for copy in loads[:2]:
        copy.wait()
    for w in (GATE, UP):
        from_sibling(w, (0, 4))
    accumulate((GATE, UP), av, (0, 4), 4, first=True)
    from_across(DOWN)
    from_x(GATE, 4)
    from_x(UP, 4)
    for w in (GATE, UP):
        from_sibling(w, (1, 2, 3))
    accumulate((GATE, UP), av, (1, 2, 3), 1)
    for w in (GATE, UP):
        from_sibling(w, (5, 6, 7))
    accumulate((GATE, UP), av, (5, 6, 7), 1)

    @pl.loop(0, ROWS // TILE)
    def _(i):
        rows = aligned(i, TILE, TILE)
        gate_pre, up_pre = pre[GATE, rows], pre[UP, rows]
        value = live_rows(i, TILE) * (gate_pre * jax.nn.sigmoid(gate_pre)) * up_pre
        af[HIDDEN, rows, my_cols] = value.astype(jnp.bfloat16)

    gathers = gather_out(HIDDEN)
    from_x(DOWN, 0)
    for copy in loads[2:]:
        copy.wait()
    finish_weight_sends(GATE)
    grad_partials(DOWN, ov, HIDDEN)
    from_sibling(DOWN, (0, 4))
    accumulate((DOWN,), ov, (0, 4), 4, first=True)
    from_x(DOWN, 4)
    from_sibling(DOWN, (1, 2, 3))
    accumulate((DOWN,), ov, (1, 2, 3), 1)
    pair_sums(DOWN)
    from_sibling(DOWN, (5, 6, 7))
    accumulate((DOWN,), ov, (5, 6, 7), 1)

    @pl.loop(0, ROWS // TILE)
    def _(i):
        rows = aligned(i, TILE, TILE)
        gate_pre, up_pre, grad_hidden = pre[GATE, rows], pre[UP, rows], pre[DOWN, rows]
        sigma = jax.nn.sigmoid(gate_pre)
        scaled = live_rows(i, TILE) * grad_hidden
        slope = sigma * (1.0 + gate_pre * (1.0 - sigma))
        af[GGP, rows, my_cols] = (scaled * up_pre * slope).astype(jnp.bfloat16)
        af[GUP, rows, my_cols] = (scaled * (gate_pre * sigma)).astype(jnp.bfloat16)

    gathers += gather_out(GGP)
    gathers += gather_out(GUP)
    finish_weight_sends(UP)
    grad_partials(GATE, av, GGP)
    finish_weight_sends(DOWN)
    grad_partials(UP, av, GUP)
    gathers += gather_forward(HIDDEN)
    pair_sums(GATE)
    pair_sums(UP)
    columns = [columns_arrived(DOWN)]
    gathers += gather_forward(GGP)
    gathers += gather_forward(GUP)
    columns.append(columns_arrived(GATE))
    columns.append(columns_arrived(UP))
    x_sums(DOWN)
    gather_done(HIDDEN)
    columns_done(DOWN)

    @pl.loop(0, ROWS // OUT_TILE)
    def _(i):
        rows = aligned(i, OUT_TILE, OUT_TILE)
        res[0, rows] = contract_last(af[HIDDEN, rows], w2[DOWN]).astype(jnp.bfloat16)

    outs = write_out(mixed, 0)
    outs.append(z_sums(DOWN))
    x_sums(GATE)
    x_sums(UP)
    gather_done(GGP)
    gather_done(GUP)
    columns_done(GATE)
    columns_done(UP)

    @pl.loop(0, ROWS // OUT_TILE)
    def _(i):
        rows = aligned(i, OUT_TILE, OUT_TILE)
        value = contract_last(af[GGP, rows], w2[GATE]) + contract_last(af[GUP, rows], w2[UP])
        res[1, rows] = value.astype(jnp.bfloat16)

    outs += write_out(input_grad, 1)
    outs.append(z_sums(GATE))
    outs.append(z_sums(UP))
    for copy in gathers + columns:
        copy.wait_send()
    for p in range(3):
        for i in range(8):
            pair_copy(p, i).wait_send()
        for i in range(6):
            x_copy(p, i).wait_send()
        z_copy(p).wait_send()
    for copy in outs:
        copy.wait()


def local(acts, counts, gate_weight, up_weight, down_weight, out_grad):
    bf16, f32 = jnp.bfloat16, jnp.float32
    dma = pltpu.SemaphoreType.DMA
    anywhere = pl.BlockSpec(memory_space=pl.ANY)
    piece = jax.ShapeDtypeStruct((2, MICRO_ROWS, CHIP), bf16)
    grad = jax.ShapeDtypeStruct((SHARD, WIDTH), f32)
    return pl.pallas_call(
        kernel,
        name="expert_layer",
        out_shape=(piece, piece, grad, grad, grad),
        in_specs=[anywhere, pl.BlockSpec(memory_space=pltpu.SMEM)] + [anywhere] * 4,
        out_specs=(anywhere,) * 5,
        scratch_shapes=[
            pltpu.VMEM((ROWS, 8 * CHIP), bf16),
            pltpu.VMEM((ROWS, 8 * CHIP), bf16),
            pltpu.VMEM((3, 8 * CHIP, WIDTH), bf16),
            pltpu.VMEM((3, CHIP, 8 * WIDTH), bf16),
            pltpu.VMEM((3, ROWS, 8 * WIDTH), bf16),
            pltpu.VMEM((3, 8, SHARD, WIDTH), bf16),
            pltpu.VMEM((3, 6, SHARD, WIDTH), bf16),
            pltpu.VMEM((3, SHARD, WIDTH), bf16),
            pltpu.VMEM((3, ROWS, WIDTH), f32),
            pltpu.VMEM((3, SHARD, WIDTH), f32),
            pltpu.VMEM((2, ROWS, CHIP), bf16),
            dma((4,)),
            dma((3,)),
            dma((3, 16)),
            dma((3, 16)),
            dma((3, 8, 2)),
            dma((3, 8, 2)),
            dma((3,)),
            dma((3,)),
            dma((3, 10)),
            dma((3, 10)),
            dma((3, 15)),
            dma((3, 15)),
            dma((7,)),
        ],
        compiler_params=pltpu.CompilerParams(
            collective_id=0, has_side_effects=True, vmem_limit_bytes=62 * 2**20
        ),
    )(acts, counts, gate_weight, up_weight, down_weight, out_grad)


def solution(mesh):
    placed = (
        P(None, "dp", None),
        P("dp", None),
        P("dp", "tensor"),
        P("dp", "tensor"),
        P("dp", "tensor"),
        P(None, "dp", None),
    )
    return jax.shard_map(
        local,
        mesh=mesh,
        in_specs=placed,
        out_specs=(
            P(None, "dp", "tensor"),
            P(None, "dp", "tensor"),
            P("dp", "tensor"),
            P("dp", "tensor"),
            P("dp", "tensor"),
        ),
        check_vma=False,
    )
```

time: 506 us -> 212 us (0.42)
  the two profiles are of different devices: /device:TPU:34 before, /device:TPU:108 now
where the time goes in v1:
time: 212 us; the launch traced here: 211 us
  Pallas kernels  201 us (95%)
  local copies, waits for them, and re-layouts  9.79 us (5%)
    pallas_call x1, Pallas kernels, local(): pl.pallas_call(kernel, name='expert_layer', out_shape=(piece, piece, grad...  201 us
    unnamed x5, local copies, waits for them, and re-layouts  9.79 us

profile of v1, /device:TPU:108, one launch (start us, length us, event | category | flops | bytes accessed | tf_op | source)
XLA Modules:
  0.0 211.4 jit_solution(4015903705794324865)
XLA Ops:
  0.6 200.9 %expert_layer.1 = (bf16[2,256,896]{2,1,0:T(8,128)(2,1)}, bf16[2,256,896]{2,1,0:T(8,128)(2,1)}, f32[448,256]{1,0:T(8,128)}, f32[448,256]{1,0:T(8,128)}, f32[448,256]{1,0:T(8,128)}) custom-call(bf16[2,256,7168]{2,1,0:T(8,128)(2,1)} %acts.1, s32[1,2]{1,0:T(1,128)} %counts.1, bf16[448,256]{1,0:T(8,128)(2,1)} %gate_w.1, bf16[448,256]{1,0:T(8,128)(2,1)} %up_w.1, ...), custom_call_target="tpu_custom_call" | custom-call | tf_op jit(solution)/shard_map/expert_layer/pallas_call | solution.py:449
  201.6 2.2 %copy.16 = bf16[2,256,896]{2,1,0:T(8,128)(2,1)} copy(bf16[2,256,896]{2,1,0:T(8,128)(2,1)} %get-tuple-element.10) | data formatting | bytes 1835008
  203.8 2.2 %copy.17 = bf16[2,256,896]{2,1,0:T(8,128)(2,1)} copy(bf16[2,256,896]{2,1,0:T(8,128)(2,1)} %get-tuple-element.11) | data formatting | bytes 1835008
  205.9 1.8 copy.18
  207.7 1.8 copy.19
  209.6 1.8 copy.20

commit v2 on v1

v2 whole, which is shorter than its diff:
```python
import jax
import jax.numpy as jnp
from jax import lax
from jax.experimental import pallas as pl
from jax.experimental.pallas import tpu as pltpu
from jax.sharding import PartitionSpec as P

MESH = pl.DeviceIdType.MESH
GATE, UP, DOWN = 0, 1, 2
HIDDEN, GGP, GUP = 0, 1, 2
SHARD = 448
CHIP = 2 * SHARD
HALF = SHARD // 2
PAIR = 2 * CHIP
WIDTH = 256
ROWS = 512
MICRO_ROWS = 256


def aligned(index, size, unit):
    return pl.ds(pl.multiple_of(index * unit, unit), size)


def contract_last(left, right):
    return lax.dot_general(left, right, (((1,), (1,)), ((), ())), preferred_element_type=jnp.float32)


def contract_first(left, right):
    return lax.dot_general(left, right, (((0,), (0,)), ((), ())), preferred_element_type=jnp.float32)


def kernel(
    acts, counts, gate_w, up_w, down_w, out_grad,
    mixed, input_grad, gate_grad, up_grad, down_grad,
    av, ov, wf, w2, af, rs, rx, rz, pre, acc,
    load_sem, own_sem, a_send, a_recv, t_send, t_recv, u_send, u_recv,
    g_send, g_recv, b_send, b_recv, out_sem,
):
    dp, t = lax.axis_index("dp"), lax.axis_index("tensor")
    x, zh, c = dp // 4, (dp // 2) % 2, dp % 2
    zl, y = t // 4, t % 4
    my_chip = x * 2 + zh
    weights = (gate_w, up_w, down_w)

    def device(dx=0, flip_zh=0, flip_c=0, flip_zl=0, dy=0):
        return (
            ((x + dx) % 4) * 4 + ((zh + flip_zh) % 2) * 2 + (c + flip_c) % 2,
            ((zl + flip_zl) % 2) * 4 + (y + dy) % 4,
        )

    def chip_of(r):
        return ((x + r % 4) % 4) * 2 + (zh + r // 4) % 2

    def remote(src, dst, send, recv, to):
        return pltpu.make_async_remote_copy(src, dst, send, recv, device_id=to, device_id_type=MESH)

    sibling = device(flip_c=1)
    across = device(flip_zh=1)
    my_cols = aligned(t, WIDTH, WIDTH)

    barrier = pltpu.get_barrier_semaphore()
    partners = [sibling, across] + [device(dx=j) for j in (1, 2, 3)]
    partners += [device(dy=j) for j in (1, 2, 3)]
    partners += [device(flip_zl=1, dy=j) for j in range(4)]
    partners += [device(flip_zl=1, flip_zh=1, dy=j) for j in range(4)]
    for to in partners:
        pl.semaphore_signal(barrier, inc=1, device_id=to, device_id_type=MESH)

    own = [pltpu.make_async_copy(weights[w], wf.at[w, aligned(dp, SHARD, SHARD)], own_sem.at[w]) for w in range(3)]
    for copy in own:
        copy.start()
    loads = []
    for which, (src, dst) in enumerate(((acts, av), (out_grad, ov))):
        for m in range(2):
            loads.append(
                pltpu.make_async_copy(
                    src.at[m], dst.at[pl.ds(m * MICRO_ROWS, MICRO_ROWS)], load_sem.at[2 * which + m]
                )
            )
    for copy in loads:
        copy.start()
    pl.semaphore_wait(barrier, len(partners))

    sends = {w: [] for w in range(3)}

    def shard_rows(r, core, low=0, size=SHARD):
        return pl.ds(pl.multiple_of((chip_of(r) * 2 + core) * SHARD + low, HALF), size)

    def move(w, r, to, index, low=0, size=SHARD):
        ref = wf.at[w, shard_rows(r, c, low, size)]
        copy = remote(ref, ref, a_send.at[w, index], a_recv.at[w, index], to)
        copy.start()
        sends[w].append(copy)

    def arrived(w, r, index, low=0, size=SHARD, core=None):
        ref = wf.at[w, shard_rows(r, c if core is None else core, low, size)]
        remote(ref, ref, a_send.at[w, index], a_recv.at[w, index], sibling).wait_recv()

    def to_sibling(w, r):
        move(w, r, sibling, 9 + r)

    def send_own(w):
        move(w, 0, across, 0)
        move(w, 0, device(dx=1), 1)
        move(w, 0, device(dx=3), 2)
        to_sibling(w, 0)

    def from_across(w):
        arrived(w, 4, 0)
        move(w, 4, device(dx=1), 3)
        move(w, 4, device(dx=3), 4)
        to_sibling(w, 4)

    def from_neighbours(w, flip):
        arrived(w, 4 * flip + 1, 2 + 2 * flip)
        move(w, 4 * flip + 1, device(dx=3), 5 + 2 * flip, 0, HALF)
        to_sibling(w, 4 * flip + 1)
        arrived(w, 4 * flip + 3, 1 + 2 * flip)
        move(w, 4 * flip + 3, device(dx=1), 6 + 2 * flip, HALF, HALF)
        to_sibling(w, 4 * flip + 3)

    def from_far(w, flip):
        arrived(w, 4 * flip + 2, 5 + 2 * flip, 0, HALF)
        arrived(w, 4 * flip + 2, 6 + 2 * flip, HALF, HALF)
        to_sibling(w, 4 * flip + 2)

    def from_sibling(w):
        for r in range(8):
            arrived(w, r, 9 + r, core=1 - c)

    def column_copy(w, to, cross, h):
        src = wf.at[w, pl.ds(pl.multiple_of((to * 2 + c) * SHARD + h * HALF, HALF), HALF)]
        dst = w2.at[w, pl.ds(pl.multiple_of(c * SHARD + h * HALF, HALF), HALF), my_cols]
        where = (x * 4 + ((zh + h * cross) % 2) * 2 + c, to)
        return remote(src, dst, t_send.at[w, to, h], t_recv.at[w, t, h], where)

    def column_stay(w):
        src = wf.at[w, pl.ds(pl.multiple_of((t * 2 + c) * SHARD, SHARD), SHARD)]
        return pltpu.make_async_copy(src, w2.at[w, aligned(c, SHARD, SHARD), my_cols], t_send.at[w, t, 0])

    ROTATION = ((0, 1), (1, 0), (0, 3), (1, 1), (0, 2), (1, 3), (1, 2))

    def column_target(flip, j):
        return ((zl + flip) % 2) * 4 + (y + j) % 4

    def columns_own(w):
        @pl.when(my_chip != t)
        def _():
            for h in range(2):
                column_copy(w, my_chip, (my_chip // 4 + zl) % 2, h).start()

    def columns_out(w):
        for flip, j in ROTATION:
            to = column_target(flip, j)

            @pl.when(to != my_chip)
            def _():
                for h in range(2):
                    column_copy(w, to, flip, h).start()

        stay = column_stay(w)
        stay.start()
        stays[w] = stay

    stays = {}

    def finish_weight_sends(w):
        for copy in sends[w]:
            copy.wait_send()
        for flip, j in ROTATION:
            for h in range(2):
                column_copy(w, column_target(flip, j), flip, h).wait_send()

    def columns_arrived(w):
        for flip, j in ROTATION:
            f = column_target(flip, j)
            for h in range(2):
                dst = w2.at[
                    w, pl.ds(pl.multiple_of(c * SHARD + h * HALF, HALF), HALF), aligned(f, WIDTH, WIDTH)
                ]
                remote(dst, dst, t_send.at[w, f, h], t_recv.at[w, f, h], sibling).wait_recv()
        mine = w2.at[w, aligned(c, SHARD, SHARD)]
        copy = remote(mine, mine, u_send.at[w], u_recv.at[w], sibling)
        copy.start()
        return copy

    def columns_done(w):
        theirs = w2.at[w, aligned(1 - c, SHARD, SHARD)]
        remote(theirs, theirs, u_send.at[w], u_recv.at[w], sibling).wait_recv()

    def accumulate(w, values):
        pre[w] = jnp.dot(values[:, 0:PAIR], wf[w, 0:PAIR], preferred_element_type=jnp.float32)

        @pl.loop(1, 4)
        def _(i):
            block = aligned(i, PAIR, PAIR)
            pre[w] += jnp.dot(values[:, block], wf[w, block], preferred_element_type=jnp.float32)

    def live_rows(i, size):
        per = MICRO_ROWS // size
        row = lax.broadcasted_iota(jnp.int32, (size, WIDTH), 0) + (i % per) * size
        return (row < counts[0, i // per]).astype(jnp.float32)

    TILE = 64

    gathers = []
    TOP, LOW = MICRO_ROWS, MICRO_ROWS // 2

    def act_ref(a, flip, k, low=0, size=ROWS):
        return af.at[a, pl.ds(low, size), aligned(((zl + flip) % 2) * 4 + (y + k) % 4, WIDTH, WIDTH)]

    def act_move(a, flip, k, to, index, low=0, size=ROWS):
        ref = act_ref(a, flip, k, low, size)
        copy = remote(ref, ref, g_send.at[a, index], g_recv.at[a, index], to)
        copy.start()
        gathers.append(copy)

    def act_arrived(a, flip, k, index, low=0, size=ROWS):
        ref = act_ref(a, flip, k, low, size)
        remote(ref, ref, g_send.at[a, index], g_recv.at[a, index], sibling).wait_recv()

    next_z = device(flip_zl=1)

    def gather_out(a):
        act_move(a, 0, 0, next_z, 0)
        act_move(a, 0, 0, device(dy=1), 1)
        act_move(a, 0, 0, device(dy=3), 2)

    def gather_near(a):
        act_arrived(a, 0, 1, 2)
        act_move(a, 0, 1, device(dy=3), 3, 0, TOP)
        act_move(a, 0, 1, next_z, 5, 0, TOP)
        act_arrived(a, 0, 3, 1)
        act_move(a, 0, 3, device(dy=1), 4, TOP, TOP)
        act_move(a, 0, 3, next_z, 6, 0, TOP)
        act_arrived(a, 1, 0, 0)
        act_move(a, 1, 0, device(dy=1), 8, TOP, TOP)
        act_move(a, 1, 0, device(dy=3), 9, TOP, TOP)

    def gather_far(a):
        act_arrived(a, 0, 2, 3, 0, TOP)
        act_move(a, 0, 2, next_z, 7, 0, TOP)
        act_arrived(a, 1, 1, 9, TOP, TOP)
        act_move(a, 1, 1, device(dy=3), 10, TOP, LOW)
        act_arrived(a, 1, 3, 8, TOP, TOP)
        act_move(a, 1, 3, device(dy=1), 11, TOP + LOW, LOW)

    def gather_done(a):
        act_arrived(a, 0, 2, 4, TOP, TOP)
        act_arrived(a, 1, 1, 5, 0, TOP)
        act_arrived(a, 1, 3, 6, 0, TOP)
        act_arrived(a, 1, 2, 7, 0, TOP)
        act_arrived(a, 1, 2, 10, TOP, LOW)
        act_arrived(a, 1, 2, 11, TOP + LOW, LOW)

    def part_at(p, index):
        if p == GATE:
            return lambda low, size: ov.at[pl.ds(low, size), aligned(index, WIDTH, WIDTH)]
        q = {DOWN: GATE, UP: UP}[p]
        return lambda low, size: wf.at[q, pl.ds(pl.multiple_of(index * SHARD + low, 16), size)]

    def dest(i):
        return ((x + 1 + i // 2) % 4) * 2 + i % 2

    def block_of(p, i, core):
        return part_at(p, dest(i) * 2 + core)(0, SHARD)

    def pair_copy(p, i):
        return remote(block_of(p, i, 1 - c), rs.at[p, i], b_send.at[p, i], b_recv.at[p, i], sibling)

    def grad_partials(p, values, a):
        @pl.loop(0, 4)
        def _(i):
            column = (x + 1 + i) % 4
            part = contract_first(values[:, aligned(column, PAIR, PAIR)], af[a, :, my_cols]).astype(jnp.bfloat16)
            for b in range(4):
                part_at(p, column * 4 + b)(0, SHARD)[...] = part[b * SHARD : (b + 1) * SHARD]
            for half in range(2):
                pair_copy(p, 2 * i + half).start()

    def x_copy(p, i):
        j, half = i // 2 + 1, i % 2
        slot = (3 - j) * 2 + half
        return remote(
            block_of(p, i, c), rx.at[p, slot], b_send.at[p, 8 + i], b_recv.at[p, 8 + slot], device(dx=j)
        )

    STEP = 112

    def pair_sums(p):
        for i in (0, 1, 4, 5, 2, 3):
            pair_copy(p, i).wait_recv()
            at = part_at(p, dest(i) * 2 + c)

            @pl.loop(0, SHARD // STEP)
            def _(s):
                low = pl.multiple_of(s * STEP, STEP)
                ref = at(low, STEP)
                total = ref[...].astype(jnp.float32) + rs[p, i, pl.ds(low, STEP)].astype(jnp.float32)
                ref[...] = total.astype(jnp.bfloat16)

            x_copy(p, i).start()

    def z_copy(p):
        src = part_at(p, (x * 2 + 1 - zh) * 2 + c)(0, SHARD)
        return remote(src, rz.at[p], b_send.at[p, 14], b_recv.at[p, 14], across)

    def x_sums(p):
        for i in (6, 7):
            pair_copy(p, i).wait_recv()
        for slot in range(6):
            remote(
                rx.at[p, slot], rx.at[p, slot], b_send.at[p, 8 + slot], b_recv.at[p, 8 + slot], sibling
            ).wait_recv()

        def total(half, low):
            inner = pl.ds(low, STEP)
            ref = part_at(p, (x * 2 + half) * 2 + c)(low, STEP)
            value = ref[...].astype(jnp.float32) + rs[p, 6 + half, inner].astype(jnp.float32)
            for k in range(3):
                value += rx[p, 2 * k + half, inner].astype(jnp.float32)
            return ref, value

        @pl.loop(0, SHARD // STEP)
        def _(s):
            ref, value = total(1 - zh, pl.multiple_of(s * STEP, STEP))
            ref[...] = value.astype(jnp.bfloat16)

        z_copy(p).start()

        @pl.loop(0, SHARD // STEP)
        def _(s):
            low = pl.multiple_of(s * STEP, STEP)
            pre[p, pl.ds(low, STEP)] = total(zh, low)[1]

    grads = {GATE: gate_grad, UP: up_grad, DOWN: down_grad}
    outs = []

    def z_sums(p):
        z_copy(p).wait_recv()

        @pl.loop(0, SHARD // STEP)
        def _(s):
            inner = aligned(s, STEP, STEP)
            pre[p, inner] += rz[p, inner].astype(jnp.float32)

        copy = pltpu.make_async_copy(pre.at[p, pl.ds(0, SHARD)], grads[p], out_sem.at[p])
        copy.start()
        outs.append(copy)

    BASE = 16 * WIDTH

    def write_out(ref, which):
        for m in range(2):
            src = ov.at[pl.ds(m * MICRO_ROWS, MICRO_ROWS), pl.ds(BASE + which * CHIP, CHIP)]
            copy = pltpu.make_async_copy(src, ref.at[m], out_sem.at[3 + 2 * which + m])
            copy.start()
            outs.append(copy)

    def columns_product(a, w, store):
        def tile(low, size):
            store(low, size, contract_last(af[a], w2[w, pl.ds(low, size)]))

        @pl.loop(0, CHIP // 256)
        def _(n):
            tile(pl.multiple_of(n * 256, 256), 256)

        tile(CHIP // 256 * 256, CHIP % 256)

    def store_mixed(low, size, value):
        ov[:, pl.ds(pl.multiple_of(BASE + low, 128), size)] = value.astype(jnp.bfloat16)

    def store_first(low, size, value):
        acc[:, pl.ds(low, size)] = value

    def store_second(low, size, value):
        total = acc[:, pl.ds(low, size)] + value
        ov[:, pl.ds(pl.multiple_of(BASE + CHIP + low, 128), size)] = total.astype(jnp.bfloat16)

    for w in range(3):
        own[w].wait()
    send_own(GATE)
    send_own(UP)
    for w in range(3):
        columns_own(w)
    from_across(GATE)
    from_neighbours(GATE, 0)
    from_across(UP)
    from_neighbours(UP, 0)
    from_neighbours(GATE, 1)
    from_far(GATE, 0)
    from_far(GATE, 1)
    columns_out(GATE)
    from_neighbours(UP, 1)
    send_own(DOWN)
    from_sibling(GATE)
    for copy in loads[:2]:
        copy.wait()
    accumulate(GATE, av)
    from_far(UP, 0)
    from_far(UP, 1)
    columns_out(UP)
    from_across(DOWN)
    from_sibling(UP)
    accumulate(UP, av)

    @pl.loop(0, ROWS // TILE)
    def _(i):
        rows = aligned(i, TILE, TILE)
        gate_pre, up_pre = pre[GATE, rows], pre[UP, rows]
        value = live_rows(i, TILE) * (gate_pre * jax.nn.sigmoid(gate_pre)) * up_pre
        af[HIDDEN, rows, my_cols] = value.astype(jnp.bfloat16)

    gather_out(HIDDEN)
    from_neighbours(DOWN, 0)
    for copy in loads[2:]:
        copy.wait()
    from_neighbours(DOWN, 1)
    finish_weight_sends(GATE)
    stays[GATE].wait()
    grad_partials(DOWN, ov, HIDDEN)
    from_far(DOWN, 0)
    from_far(DOWN, 1)
    columns_out(DOWN)
    from_sibling(DOWN)
    accumulate(DOWN, ov)

    @pl.loop(0, ROWS // TILE)
    def _(i):
        rows = aligned(i, TILE, TILE)
        gate_pre, up_pre, grad_hidden = pre[GATE, rows], pre[UP, rows], pre[DOWN, rows]
        sigma = jax.nn.sigmoid(gate_pre)
        scaled = live_rows(i, TILE) * grad_hidden
        slope = sigma * (1.0 + gate_pre * (1.0 - sigma))
        af[GGP, rows, my_cols] = (scaled * up_pre * slope).astype(jnp.bfloat16)
        af[GUP, rows, my_cols] = (scaled * (gate_pre * sigma)).astype(jnp.bfloat16)

    gather_out(GGP)
    gather_out(GUP)
    pair_sums(DOWN)
    grad_partials(GATE, av, GGP)
    gather_near(HIDDEN)
    finish_weight_sends(UP)
    stays[UP].wait()
    grad_partials(UP, av, GUP)
    pair_sums(GATE)
    gather_far(HIDDEN)
    pair_sums(UP)
    columns = [columns_arrived(GATE), columns_arrived(UP)]
    x_sums(DOWN)
    gather_near(GGP)
    stays[DOWN].wait()
    columns.append(columns_arrived(DOWN))
    gather_near(GUP)
    gather_done(HIDDEN)
    gather_far(GGP)
    gather_far(GUP)
    columns_done(DOWN)
    columns_product(HIDDEN, DOWN, store_mixed)
    write_out(mixed, 0)
    z_sums(DOWN)
    x_sums(GATE)
    gather_done(GGP)
    columns_done(GATE)
    columns_product(GGP, GATE, store_first)
    x_sums(UP)
    gather_done(GUP)
    columns_done(UP)
    columns_product(GUP, UP, store_second)
    write_out(input_grad, 1)
    z_sums(GATE)
    z_sums(UP)
    finish_weight_sends(DOWN)
    for copy in gathers + columns:
        copy.wait_send()
    for p in range(3):
        for i in range(8):
            pair_copy(p, i).wait_send()
        for i in range(6):
            x_copy(p, i).wait_send()
        z_copy(p).wait_send()
    for copy in outs:
        copy.wait()


def hand_on(*refs):
    sources, targets, held, in_sem, out_sem = refs[:5], refs[5:10], refs[10:15], refs[15], refs[16]
    copies_in = [pltpu.make_async_copy(sources[i], held[i], in_sem.at[i]) for i in range(5)]
    copies_out = [pltpu.make_async_copy(held[i], targets[i], out_sem.at[i]) for i in range(5)]
    for copy in copies_in:
        copy.start()
    for i in range(5):
        copies_in[i].wait()
        copies_out[i].start()
    for copy in copies_out:
        copy.wait()


def local(acts, counts, gate_weight, up_weight, down_weight, out_grad):
    bf16, f32 = jnp.bfloat16, jnp.float32
    dma = pltpu.SemaphoreType.DMA
    anywhere = pl.BlockSpec(memory_space=pl.ANY)
    piece = jax.ShapeDtypeStruct((2, MICRO_ROWS, CHIP), bf16)
    grad = jax.ShapeDtypeStruct((SHARD, WIDTH), f32)
    outs = pl.pallas_call(
        kernel,
        name="expert_layer",
        out_shape=(piece, piece, grad, grad, grad),
        in_specs=[anywhere, pl.BlockSpec(memory_space=pltpu.SMEM)] + [anywhere] * 4,
        out_specs=(anywhere,) * 5,
        scratch_shapes=[
            pltpu.VMEM((ROWS, 8 * CHIP), bf16),
            pltpu.VMEM((ROWS, 8 * CHIP), bf16),
            pltpu.VMEM((3, 8 * CHIP, WIDTH), bf16),
            pltpu.VMEM((3, CHIP, 8 * WIDTH), bf16),
            pltpu.VMEM((3, ROWS, 8 * WIDTH), bf16),
            pltpu.VMEM((3, 8, SHARD, WIDTH), bf16),
            pltpu.VMEM((3, 6, SHARD, WIDTH), bf16),
            pltpu.VMEM((3, SHARD, WIDTH), bf16),
            pltpu.VMEM((3, ROWS, WIDTH), f32),
            pltpu.VMEM((ROWS, CHIP), f32),
            dma((4,)),
            dma((3,)),
            dma((3, 17)),
            dma((3, 17)),
            dma((3, 8, 2)),
            dma((3, 8, 2)),
            dma((3,)),
            dma((3,)),
            dma((3, 12)),
            dma((3, 12)),
            dma((3, 15)),
            dma((3, 15)),
            dma((7,)),
        ],
        compiler_params=pltpu.CompilerParams(
            collective_id=0, has_side_effects=True, vmem_limit_bytes=62 * 2**20
        ),
    )(acts, counts, gate_weight, up_weight, down_weight, out_grad)
    return pl.pallas_call(
        hand_on,
        name="hand_on",
        out_shape=(piece, piece, grad, grad, grad),
        in_specs=[anywhere] * 5,
        out_specs=(anywhere,) * 5,
        scratch_shapes=[pltpu.VMEM(leaf.shape, leaf.dtype) for leaf in (piece, piece, grad, grad, grad)]
        + [dma((5,)), dma((5,))],
    )(*outs)


def solution(mesh):
    placed = (
        P(None, "dp", None),
        P("dp", None),
        P("dp", "tensor"),
        P("dp", "tensor"),
        P("dp", "tensor"),
        P(None, "dp", None),
    )
    return jax.shard_map(
        local,
        mesh=mesh,
        in_specs=placed,
        out_specs=(
            P(None, "dp", "tensor"),
            P(None, "dp", "tensor"),
            P("dp", "tensor"),
            P("dp", "tensor"),
            P("dp", "tensor"),
        ),
        check_vma=False,
    )
```

time: 212 us -> 179 us (0.84)
  the two profiles are of different devices: /device:TPU:108 before, /device:TPU:34 now
where the time goes in v2:
time: 179 us; the launch traced here: 176 us
  Pallas kernels  176 us (98%)
    pallas_call x1, Pallas kernels, local(): pl.pallas_call(kernel, name='expert_layer', out_shape=(piece, piece, grad...  173 us

profile of v2, /device:TPU:34, one launch (start us, length us, event | category | flops | bytes accessed | tf_op | source)
XLA Modules:
  0.0 176.4 jit_solution(3392601181840844190)
XLA Ops:
  0.6 172.8 %expert_layer.1 = (bf16[2,256,896]{2,1,0:T(8,128)(2,1)}, bf16[2,256,896]{2,1,0:T(8,128)(2,1)}, f32[448,256]{1,0:T(8,128)}, f32[448,256]{1,0:T(8,128)}, f32[448,256]{1,0:T(8,128)}) custom-call(bf16[2,256,7168]{2,1,0:T(8,128)(2,1)} %acts.1, s32[1,2]{1,0:T(1,128)} %counts.1, bf16[448,256]{1,0:T(8,128)(2,1)} %gate_w.1, bf16[448,256]{1,0:T(8,128)(2,1)} %up_w.1, ...), custom_call_target="tpu_custom_call" | custom-call | tf_op jit(solution)/shard_map/expert_layer/pallas_call | solution.py:505
  173.5 2.9 %hand_on.1 = (bf16[2,256,896]{2,1,0:T(8,128)(2,1)}, bf16[2,256,896]{2,1,0:T(8,128)(2,1)}, f32[448,256]{1,0:T(8,128)}, f32[448,256]{1,0:T(8,128)}, f32[448,256]{1,0:T(8,128)}) custom-call(bf16[2,256,896]{2,1,0:T(8,128)(2,1)} %get-tuple-element.10.refs_0_, bf16[2,256,896]{2,1,0:T(8,128)(2,1)} %get-tuple-element.11.refs_1_, ...), custom_call_target="tpu_custom_call" | custom-call | tf_op jit(solution)/shard_map/hand_on/pallas_call | solution.py:540

commit v3 on v2

--- a/solution.py
+++ b/solution.py
@@ -32,7 +32,7 @@
 def kernel(
     acts, counts, gate_w, up_w, down_w, out_grad,
     mixed, input_grad, gate_grad, up_grad, down_grad,
-    av, ov, wf, w2, af, rs, rx, rz, pre, acc,
+    av, ov, wf, w2, af, rs, rx, rz, pre, acc, pd,
     load_sem, own_sem, a_send, a_recv, t_send, t_recv, u_send, u_recv,
     g_send, g_recv, b_send, b_recv, out_sem,
 ):
@@ -143,26 +143,18 @@
     def column_target(flip, j):
         return ((zl + flip) % 2) * 4 + (y + j) % 4
 
-    def columns_own(w):
-        @pl.when(my_chip != t)
-        def _():
-            for h in range(2):
-                column_copy(w, my_chip, (my_chip // 4 + zl) % 2, h).start()
-
-    def columns_out(w):
-        for flip, j in ROTATION:
-            to = column_target(flip, j)
-
-            @pl.when(to != my_chip)
+    def columns_out(w, relations):
+        for r in relations:
+            to = chip_of(r)
+
+            @pl.when(to != t)
             def _():
                 for h in range(2):
-                    column_copy(w, to, flip, h).start()
-
-        stay = column_stay(w)
-        stay.start()
-        stays[w] = stay
-
-    stays = {}
+                    column_copy(w, to, (to // 4 + zl) % 2, h).start()
+
+            @pl.when(to == t)
+            def _():
+                column_stay(w).start()
 
     def finish_weight_sends(w):
         for copy in sends[w]:
@@ -256,8 +248,8 @@
     def part_at(p, index):
         if p == GATE:
             return lambda low, size: ov.at[pl.ds(low, size), aligned(index, WIDTH, WIDTH)]
-        q = {DOWN: GATE, UP: UP}[p]
-        return lambda low, size: wf.at[q, pl.ds(pl.multiple_of(index * SHARD + low, 16), size)]
+        held = pd if p == DOWN else wf.at[GATE]
+        return lambda low, size: held.at[pl.ds(pl.multiple_of(index * SHARD + low, 16), size)]
 
     def dest(i):
         return ((x + 1 + i // 2) % 4) * 2 + i % 2
@@ -377,30 +369,35 @@
         total = acc[:, pl.ds(low, size)] + value
         ov[:, pl.ds(pl.multiple_of(BASE + CHIP + low, 128), size)] = total.astype(jnp.bfloat16)
 
+    NEAR, FAR = (4, 1, 3), (5, 7, 2, 6)
     for w in range(3):
         own[w].wait()
     send_own(GATE)
-    send_own(UP)
-    for w in range(3):
-        columns_own(w)
+    columns_out(GATE, (0,))
     from_across(GATE)
     from_neighbours(GATE, 0)
+    send_own(UP)
+    columns_out(GATE, NEAR)
+    from_neighbours(GATE, 1)
+    columns_out(UP, (0,))
     from_across(UP)
-    from_neighbours(UP, 0)
-    from_neighbours(GATE, 1)
     from_far(GATE, 0)
     from_far(GATE, 1)
-    columns_out(GATE)
-    from_neighbours(UP, 1)
+    columns_out(GATE, FAR)
+    from_neighbours(UP, 0)
     send_own(DOWN)
+    columns_out(UP, NEAR)
+    columns_out(DOWN, (0,))
     from_sibling(GATE)
     for copy in loads[:2]:
         copy.wait()
     accumulate(GATE, av)
+    from_neighbours(UP, 1)
+    from_across(DOWN)
     from_far(UP, 0)
     from_far(UP, 1)
-    columns_out(UP)
-    from_across(DOWN)
+    columns_out(UP, FAR)
+    from_neighbours(DOWN, 0)
     from_sibling(UP)
     accumulate(UP, av)
 
@@ -412,16 +409,15 @@
         af[HIDDEN, rows, my_cols] = value.astype(jnp.bfloat16)
 
     gather_out(HIDDEN)
-    from_neighbours(DOWN, 0)
+    columns_out(DOWN, NEAR)
+    from_neighbours(DOWN, 1)
     for copy in loads[2:]:
         copy.wait()
-    from_neighbours(DOWN, 1)
-    finish_weight_sends(GATE)
-    stays[GATE].wait()
     grad_partials(DOWN, ov, HIDDEN)
     from_far(DOWN, 0)
     from_far(DOWN, 1)
-    columns_out(DOWN)
+    columns_out(DOWN, FAR)
+    pair_sums(DOWN)
     from_sibling(DOWN)
     accumulate(DOWN, ov)
 
@@ -437,27 +433,28 @@
 
     gather_out(GGP)
     gather_out(GUP)
-    pair_sums(DOWN)
     grad_partials(GATE, av, GGP)
+    finish_weight_sends(GATE)
+    column_stay(GATE).wait()
+    grad_partials(UP, av, GUP)
     gather_near(HIDDEN)
-    finish_weight_sends(UP)
-    stays[UP].wait()
-    grad_partials(UP, av, GUP)
     pair_sums(GATE)
     gather_far(HIDDEN)
     pair_sums(UP)
-    columns = [columns_arrived(GATE), columns_arrived(UP)]
+    columns = [columns_arrived(GATE)]
+    column_stay(UP).wait()
+    columns.append(columns_arrived(UP))
     x_sums(DOWN)
     gather_near(GGP)
-    stays[DOWN].wait()
+    column_stay(DOWN).wait()
     columns.append(columns_arrived(DOWN))
     gather_near(GUP)
+    gather_far(GGP)
     gather_done(HIDDEN)
-    gather_far(GGP)
-    gather_far(GUP)
     columns_done(DOWN)
     columns_product(HIDDEN, DOWN, store_mixed)
     write_out(mixed, 0)
+    gather_far(GUP)
     z_sums(DOWN)
     x_sums(GATE)
     gather_done(GGP)
@@ -470,6 +467,7 @@
     write_out(input_grad, 1)
     z_sums(GATE)
     z_sums(UP)
+    finish_weight_sends(UP)
     finish_weight_sends(DOWN)
     for copy in gathers + columns:
         copy.wait_send()
@@ -519,6 +517,7 @@
             pltpu.VMEM((3, SHARD, WIDTH), bf16),
             pltpu.VMEM((3, ROWS, WIDTH), f32),
             pltpu.VMEM((ROWS, CHIP), f32),
+            pltpu.VMEM((8 * CHIP, WIDTH), bf16),
             dma((4,)),
             dma((3,)),
             dma((3, 17)),

time: 179 us -> 157 us (0.88); the launches traced: 176 us -> 157 us
  Pallas kernels: 176 us -> 156 us
    pallas_call x1, Pallas kernels: 173 us -> 153 us  [local(): pl.pallas_call(kernel, name='expert_layer', out_shape=(piece, piece, grad...]
where the time goes in v3:
time: 157 us
  Pallas kernels  156 us (99%)
    pallas_call x1, Pallas kernels, local(): pl.pallas_call(kernel, name='expert_layer', out_shape=(piece, piece, grad...  153 us

profile of v3, /device:TPU:34, one launch (start us, length us, event | category | flops | bytes accessed | tf_op | source)
XLA Modules:
  0.0 156.8 jit_solution(6317050477838470305)
XLA Ops:
  0.6 153.0 %expert_layer.1 = (bf16[2,256,896]{2,1,0:T(8,128)(2,1)}, bf16[2,256,896]{2,1,0:T(8,128)(2,1)}, f32[448,256]{1,0:T(8,128)}, f32[448,256]{1,0:T(8,128)}, f32[448,256]{1,0:T(8,128)}) custom-call(bf16[2,256,7168]{2,1,0:T(8,128)(2,1)} %acts.1, s32[1,2]{1,0:T(1,128)} %counts.1, bf16[448,256]{1,0:T(8,128)(2,1)} %gate_w.1, bf16[448,256]{1,0:T(8,128)(2,1)} %up_w.1, ...), custom_call_target="tpu_custom_call" | custom-call | tf_op jit(solution)/shard_map/expert_layer/pallas_call | solution.py:503
  153.7 2.9 %hand_on.1 = (bf16[2,256,896]{2,1,0:T(8,128)(2,1)}, bf16[2,256,896]{2,1,0:T(8,128)(2,1)}, f32[448,256]{1,0:T(8,128)}, f32[448,256]{1,0:T(8,128)}, f32[448,256]{1,0:T(8,128)}) custom-call(bf16[2,256,896]{2,1,0:T(8,128)(2,1)} %get-tuple-element.10.refs_0_, bf16[2,256,896]{2,1,0:T(8,128)(2,1)} %get-tuple-element.11.refs_1_, ...), custom_call_target="tpu_custom_call" | custom-call | tf_op jit(solution)/shard_map/hand_on/pallas_call | solution.py:539

commit v4 on v3

--- a/solution.py
+++ b/solution.py
@@ -33,7 +33,7 @@
     acts, counts, gate_w, up_w, down_w, out_grad,
     mixed, input_grad, gate_grad, up_grad, down_grad,
     av, ov, wf, w2, af, rs, rx, rz, pre, acc, pd,
-    load_sem, own_sem, a_send, a_recv, t_send, t_recv, u_send, u_recv,
+    load_sem, own_sem, a_send, a_recv, t_send, t_recv, u_send, u_recv, v_send, v_recv,
     g_send, g_recv, b_send, b_recv, out_sem,
 ):
     dp, t = lax.axis_index("dp"), lax.axis_index("tensor")
@@ -99,8 +99,10 @@
     def to_sibling(w, r):
         move(w, r, sibling, 9 + r)
 
+    def send_across(w):
+        move(w, 0, across, 0)
+
     def send_own(w):
-        move(w, 0, across, 0)
         move(w, 0, device(dx=1), 1)
         move(w, 0, device(dx=3), 2)
         to_sibling(w, 0)
@@ -128,15 +130,26 @@
         for r in range(8):
             arrived(w, r, 9 + r, core=1 - c)
 
+    def piece_rows(w, h):
+        if w == DOWN:
+            return (x % 2) * HALF + h * (HALF // 2), HALF // 2
+        return h * HALF, HALF
+
+    def column_rows(w, base, h):
+        low, size = piece_rows(w, h)
+        return pl.ds(pl.multiple_of(base * SHARD + low, HALF // 2), size)
+
     def column_copy(w, to, cross, h):
-        src = wf.at[w, pl.ds(pl.multiple_of((to * 2 + c) * SHARD + h * HALF, HALF), HALF)]
-        dst = w2.at[w, pl.ds(pl.multiple_of(c * SHARD + h * HALF, HALF), HALF), my_cols]
+        src = wf.at[w, column_rows(w, to * 2 + c, h)]
+        dst = w2.at[w, column_rows(w, c, h), my_cols]
         where = (x * 4 + ((zh + h * cross) % 2) * 2 + c, to)
         return remote(src, dst, t_send.at[w, to, h], t_recv.at[w, t, h], where)
 
     def column_stay(w):
-        src = wf.at[w, pl.ds(pl.multiple_of((t * 2 + c) * SHARD, SHARD), SHARD)]
-        return pltpu.make_async_copy(src, w2.at[w, aligned(c, SHARD, SHARD), my_cols], t_send.at[w, t, 0])
+        low, size = ((x % 2) * HALF, HALF) if w == DOWN else (0, SHARD)
+        src = wf.at[w, pl.ds(pl.multiple_of((t * 2 + c) * SHARD + low, HALF), size)]
+        dst = w2.at[w, pl.ds(pl.multiple_of(c * SHARD + low, HALF), size), my_cols]
+        return pltpu.make_async_copy(src, dst, t_send.at[w, t, 0])
 
     ROTATION = ((0, 1), (1, 0), (0, 3), (1, 1), (0, 2), (1, 3), (1, 2))
 
@@ -163,19 +176,44 @@
             for h in range(2):
                 column_copy(w, column_target(flip, j), flip, h).wait_send()
 
-    def columns_arrived(w):
+    def columns_in(w):
+        column_stay(w).wait()
         for flip, j in ROTATION:
             f = column_target(flip, j)
             for h in range(2):
-                dst = w2.at[
-                    w, pl.ds(pl.multiple_of(c * SHARD + h * HALF, HALF), HALF), aligned(f, WIDTH, WIDTH)
-                ]
+                dst = w2.at[w, column_rows(w, c, h), aligned(f, WIDTH, WIDTH)]
                 remote(dst, dst, t_send.at[w, f, h], t_recv.at[w, f, h], sibling).wait_recv()
+
+    def columns_pair(w):
         mine = w2.at[w, aligned(c, SHARD, SHARD)]
         copy = remote(mine, mine, u_send.at[w], u_recv.at[w], sibling)
         copy.start()
         return copy
 
+    def columns_arrived(w):
+        columns_in(w)
+        return columns_pair(w)
+
+    def quarter(parity, q):
+        low = c * SHARD + parity * HALF + q * (HALF // 2)
+        return w2.at[DOWN, pl.ds(pl.multiple_of(low, HALF // 2), HALF // 2)]
+
+    def quarters_out():
+        columns_in(DOWN)
+        out = []
+        for q in range(2):
+            ref = quarter(x % 2, q)
+            copy = remote(ref, ref, v_send.at[q], v_recv.at[q], device(dx=3 - 2 * q))
+            copy.start()
+            out.append(copy)
+        return out
+
+    def quarters_in():
+        for q in range(2):
+            ref = quarter(1 - x % 2, q)
+            remote(ref, ref, v_send.at[q], v_recv.at[q], sibling).wait_recv()
+        return columns_pair(DOWN)
+
     def columns_done(w):
         theirs = w2.at[w, aligned(1 - c, SHARD, SHARD)]
         remote(theirs, theirs, u_send.at[w], u_recv.at[w], sibling).wait_recv()
@@ -196,7 +234,8 @@
     TILE = 64
 
     gathers = []
-    TOP, LOW = MICRO_ROWS, MICRO_ROWS // 2
+    MIDDLE, TOP = ROWS // 2, 256
+    LOW = (ROWS - TOP) // 2
 
     def act_ref(a, flip, k, low=0, size=ROWS):
         return af.at[a, pl.ds(low, size), aligned(((zl + flip) % 2) * 4 + (y + k) % 4, WIDTH, WIDTH)]
@@ -220,25 +259,25 @@
 
     def gather_near(a):
         act_arrived(a, 0, 1, 2)
-        act_move(a, 0, 1, device(dy=3), 3, 0, TOP)
+        act_move(a, 0, 1, device(dy=3), 3, 0, MIDDLE)
         act_move(a, 0, 1, next_z, 5, 0, TOP)
         act_arrived(a, 0, 3, 1)
-        act_move(a, 0, 3, device(dy=1), 4, TOP, TOP)
+        act_move(a, 0, 3, device(dy=1), 4, MIDDLE, ROWS - MIDDLE)
         act_move(a, 0, 3, next_z, 6, 0, TOP)
         act_arrived(a, 1, 0, 0)
-        act_move(a, 1, 0, device(dy=1), 8, TOP, TOP)
-        act_move(a, 1, 0, device(dy=3), 9, TOP, TOP)
+        act_move(a, 1, 0, device(dy=1), 8, TOP, ROWS - TOP)
+        act_move(a, 1, 0, device(dy=3), 9, TOP, ROWS - TOP)
 
     def gather_far(a):
-        act_arrived(a, 0, 2, 3, 0, TOP)
+        act_arrived(a, 0, 2, 3, 0, MIDDLE)
         act_move(a, 0, 2, next_z, 7, 0, TOP)
-        act_arrived(a, 1, 1, 9, TOP, TOP)
+        act_arrived(a, 1, 1, 9, TOP, ROWS - TOP)
         act_move(a, 1, 1, device(dy=3), 10, TOP, LOW)
-        act_arrived(a, 1, 3, 8, TOP, TOP)
+        act_arrived(a, 1, 3, 8, TOP, ROWS - TOP)
         act_move(a, 1, 3, device(dy=1), 11, TOP + LOW, LOW)
 
     def gather_done(a):
-        act_arrived(a, 0, 2, 4, TOP, TOP)
+        act_arrived(a, 0, 2, 4, MIDDLE, ROWS - MIDDLE)
         act_arrived(a, 1, 1, 5, 0, TOP)
         act_arrived(a, 1, 3, 6, 0, TOP)
         act_arrived(a, 1, 2, 7, 0, TOP)
@@ -270,17 +309,28 @@
             for half in range(2):
                 pair_copy(p, 2 * i + half).start()
 
-    def x_copy(p, i):
-        j, half = i // 2 + 1, i % 2
-        slot = (3 - j) * 2 + half
+    def along(s):
+        return device(dx=1 + 2 * s)
+
+    def far_copy(p, s, half):
+        src = part_at(p, (((x + 2) % 4) * 2 + half) * 2 + c)(s * HALF, HALF)
+        index = 8 + 2 * s + half
         return remote(
-            block_of(p, i, c), rx.at[p, slot], b_send.at[p, 8 + i], b_recv.at[p, 8 + slot], device(dx=j)
+            src, rx.at[p, 4 + s, pl.ds(half * HALF, HALF)], b_send.at[p, index], b_recv.at[p, index], along(s)
         )
 
+    def near_copy(p, s, half, relayed):
+        low = (s if relayed else 1 - s) * HALF
+        src = part_at(p, (((x + 1 + 2 * s) % 4) * 2 + half) * 2 + c)(low, HALF)
+        index = 12 + 4 * s + 2 * half + relayed
+        return remote(
+            src, rx.at[p, 2 * s + half, pl.ds(low, HALF)], b_send.at[p, index], b_recv.at[p, index], along(s)
+        )
+
     STEP = 112
 
     def pair_sums(p):
-        for i in (0, 1, 4, 5, 2, 3):
+        for i in (2, 3, 0, 1, 4, 5):
             pair_copy(p, i).wait_recv()
             at = part_at(p, dest(i) * 2 + c)
 
@@ -291,25 +341,45 @@
                 total = ref[...].astype(jnp.float32) + rs[p, i, pl.ds(low, STEP)].astype(jnp.float32)
                 ref[...] = total.astype(jnp.bfloat16)
 
-            x_copy(p, i).start()
+            j, half = i // 2 + 1, i % 2
+            if j == 2:
+                far_copy(p, 0, half).start()
+                far_copy(p, 1, half).start()
+            else:
+                near_copy(p, j // 2, half, 0).start()
+
+    def far_sums(p):
+        for half in range(2):
+            for s in range(2):
+                far_copy(p, s, half).wait_recv()
+                at = part_at(p, (((x + 1 + 2 * s) % 4) * 2 + half) * 2 + c)
+
+                @pl.loop(0, HALF // STEP)
+                def _(i):
+                    low = pl.multiple_of(i * STEP, STEP)
+                    ref = at(s * HALF + low, STEP)
+                    more = rx[p, 4 + s, pl.ds(half * HALF + low, STEP)]
+                    ref[...] = (ref[...].astype(jnp.float32) + more.astype(jnp.float32)).astype(jnp.bfloat16)
+
+                near_copy(p, s, half, 1).start()
 
     def z_copy(p):
         src = part_at(p, (x * 2 + 1 - zh) * 2 + c)(0, SHARD)
-        return remote(src, rz.at[p], b_send.at[p, 14], b_recv.at[p, 14], across)
+        return remote(src, rz.at[p], b_send.at[p, 20], b_recv.at[p, 20], across)
 
     def x_sums(p):
         for i in (6, 7):
             pair_copy(p, i).wait_recv()
-        for slot in range(6):
-            remote(
-                rx.at[p, slot], rx.at[p, slot], b_send.at[p, 8 + slot], b_recv.at[p, 8 + slot], sibling
-            ).wait_recv()
+        for half in range(2):
+            for s in range(2):
+                for relayed in range(2):
+                    near_copy(p, s, half, relayed).wait_recv()
 
         def total(half, low):
             inner = pl.ds(low, STEP)
             ref = part_at(p, (x * 2 + half) * 2 + c)(low, STEP)
             value = ref[...].astype(jnp.float32) + rs[p, 6 + half, inner].astype(jnp.float32)
-            for k in range(3):
+            for k in range(2):
                 value += rx[p, 2 * k + half, inner].astype(jnp.float32)
             return ref, value
 
@@ -372,7 +442,10 @@
     NEAR, FAR = (4, 1, 3), (5, 7, 2, 6)
     for w in range(3):
         own[w].wait()
+    send_across(GATE)
     send_own(GATE)
+    send_across(UP)
+    send_across(DOWN)
     columns_out(GATE, (0,))
     from_across(GATE)
     from_neighbours(GATE, 0)
@@ -387,7 +460,6 @@
     from_neighbours(UP, 0)
     send_own(DOWN)
     columns_out(UP, NEAR)
-    columns_out(DOWN, (0,))
     from_sibling(GATE)
     for copy in loads[:2]:
         copy.wait()
@@ -409,14 +481,12 @@
         af[HIDDEN, rows, my_cols] = value.astype(jnp.bfloat16)
 
     gather_out(HIDDEN)
-    columns_out(DOWN, NEAR)
     from_neighbours(DOWN, 1)
     for copy in loads[2:]:
         copy.wait()
     grad_partials(DOWN, ov, HIDDEN)
     from_far(DOWN, 0)
     from_far(DOWN, 1)
-    columns_out(DOWN, FAR)
     pair_sums(DOWN)
     from_sibling(DOWN)
     accumulate(DOWN, ov)
@@ -433,39 +503,41 @@
 
     gather_out(GGP)
     gather_out(GUP)
+    columns_out(DOWN, (0,) + NEAR + FAR)
     grad_partials(GATE, av, GGP)
+    far_sums(DOWN)
     finish_weight_sends(GATE)
-    column_stay(GATE).wait()
+    columns = [columns_arrived(GATE)]
     grad_partials(UP, av, GUP)
     gather_near(HIDDEN)
     pair_sums(GATE)
     gather_far(HIDDEN)
     pair_sums(UP)
-    columns = [columns_arrived(GATE)]
-    column_stay(UP).wait()
+    far_sums(GATE)
+    gather_near(GGP)
     columns.append(columns_arrived(UP))
+    gather_near(GUP)
     x_sums(DOWN)
-    gather_near(GGP)
-    column_stay(DOWN).wait()
-    columns.append(columns_arrived(DOWN))
-    gather_near(GUP)
+    far_sums(UP)
+    columns += quarters_out()
     gather_far(GGP)
+    gather_far(GUP)
     gather_done(HIDDEN)
-    columns_done(DOWN)
-    columns_product(HIDDEN, DOWN, store_mixed)
-    write_out(mixed, 0)
-    gather_far(GUP)
     z_sums(DOWN)
     x_sums(GATE)
     gather_done(GGP)
     columns_done(GATE)
     columns_product(GGP, GATE, store_first)
-    x_sums(UP)
+    columns.append(quarters_in())
     gather_done(GUP)
     columns_done(UP)
     columns_product(GUP, UP, store_second)
     write_out(input_grad, 1)
+    x_sums(UP)
     z_sums(GATE)
+    columns_done(DOWN)
+    columns_product(HIDDEN, DOWN, store_mixed)
+    write_out(mixed, 0)
     z_sums(UP)
     finish_weight_sends(UP)
     finish_weight_sends(DOWN)
@@ -474,8 +546,11 @@
     for p in range(3):
         for i in range(8):
             pair_copy(p, i).wait_send()
-        for i in range(6):
-            x_copy(p, i).wait_send()
+        for half in range(2):
+            for s in range(2):
+                far_copy(p, s, half).wait_send()
+                near_copy(p, s, half, 0).wait_send()
+                near_copy(p, s, half, 1).wait_send()
         z_copy(p).wait_send()
     for copy in outs:
         copy.wait()
@@ -526,10 +601,12 @@
             dma((3, 8, 2)),
             dma((3,)),
             dma((3,)),
+            dma((2,)),
+            dma((2,)),
             dma((3, 12)),
             dma((3, 12)),
-            dma((3, 15)),
-            dma((3, 15)),
+            dma((3, 21)),
+            dma((3, 21)),
             dma((7,)),
         ],
         compiler_params=pltpu.CompilerParams(

time: 157 us -> 151 us (0.962)
  the two profiles are of different devices: /device:TPU:34 before, /device:TPU:64 now
where the time goes in v4:
time: 151 us
  Pallas kernels  150 us (99%)
    pallas_call x1, Pallas kernels, local(): pl.pallas_call(kernel, name='expert_layer', out_shape=(piece, piece, grad...  148 us

profile of v4, /device:TPU:64, one launch (start us, length us, event | category | flops | bytes accessed | tf_op | source)
XLA Modules:
  0.0 151.3 jit_solution(7539527289066835242)
XLA Ops:
  0.6 147.5 %expert_layer.1 = (bf16[2,256,896]{2,1,0:T(8,128)(2,1)}, bf16[2,256,896]{2,1,0:T(8,128)(2,1)}, f32[448,256]{1,0:T(8,128)}, f32[448,256]{1,0:T(8,128)}, f32[448,256]{1,0:T(8,128)}) custom-call(bf16[2,256,7168]{2,1,0:T(8,128)(2,1)} %acts.1, s32[1,2]{1,0:T(1,128)} %counts.1, bf16[448,256]{1,0:T(8,128)(2,1)} %gate_w.1, bf16[448,256]{1,0:T(8,128)(2,1)} %up_w.1, ...), custom_call_target="tpu_custom_call" | custom-call | tf_op jit(solution)/shard_map/expert_layer/pallas_call | solution.py:578
  148.2 2.9 %hand_on.1 = (bf16[2,256,896]{2,1,0:T(8,128)(2,1)}, bf16[2,256,896]{2,1,0:T(8,128)(2,1)}, f32[448,256]{1,0:T(8,128)}, f32[448,256]{1,0:T(8,128)}, f32[448,256]{1,0:T(8,128)}) custom-call(bf16[2,256,896]{2,1,0:T(8,128)(2,1)} %get-tuple-element.10.refs_0_, bf16[2,256,896]{2,1,0:T(8,128)(2,1)} %get-tuple-element.11.refs_1_, ...), custom_call_target="tpu_custom_call" | custom-call | tf_op jit(solution)/shard_map/hand_on/pallas_call | solution.py:616

commit v5 on v4

--- a/solution.py
+++ b/solution.py
@@ -258,15 +258,15 @@
         act_move(a, 0, 0, device(dy=3), 2)
 
     def gather_near(a):
+        act_arrived(a, 1, 0, 0)
+        act_move(a, 1, 0, device(dy=1), 8, TOP, ROWS - TOP)
+        act_move(a, 1, 0, device(dy=3), 9, TOP, ROWS - TOP)
         act_arrived(a, 0, 1, 2)
         act_move(a, 0, 1, device(dy=3), 3, 0, MIDDLE)
         act_move(a, 0, 1, next_z, 5, 0, TOP)
         act_arrived(a, 0, 3, 1)
         act_move(a, 0, 3, device(dy=1), 4, MIDDLE, ROWS - MIDDLE)
         act_move(a, 0, 3, next_z, 6, 0, TOP)
-        act_arrived(a, 1, 0, 0)
-        act_move(a, 1, 0, device(dy=1), 8, TOP, ROWS - TOP)
-        act_move(a, 1, 0, device(dy=3), 9, TOP, ROWS - TOP)
 
     def gather_far(a):
         act_arrived(a, 0, 2, 3, 0, MIDDLE)
@@ -503,25 +503,25 @@
 
     gather_out(GGP)
     gather_out(GUP)
-    columns_out(DOWN, (0,) + NEAR + FAR)
     grad_partials(GATE, av, GGP)
     far_sums(DOWN)
+    gather_near(HIDDEN)
     finish_weight_sends(GATE)
     columns = [columns_arrived(GATE)]
     grad_partials(UP, av, GUP)
-    gather_near(HIDDEN)
     pair_sums(GATE)
     gather_far(HIDDEN)
+    gather_near(GGP)
+    columns_out(DOWN, (0,) + NEAR + FAR)
     pair_sums(UP)
+    gather_near(GUP)
     far_sums(GATE)
-    gather_near(GGP)
+    gather_far(GGP)
     columns.append(columns_arrived(UP))
-    gather_near(GUP)
+    far_sums(UP)
+    gather_far(GUP)
+    columns += quarters_out()
     x_sums(DOWN)
-    far_sums(UP)
-    columns += quarters_out()
-    gather_far(GGP)
-    gather_far(GUP)
     gather_done(HIDDEN)
     z_sums(DOWN)
     x_sums(GATE)

time: 151 us -> 149 us (0.987)
  the two profiles are of different devices: /device:TPU:64 before, /device:TPU:34 now
where the time goes in v5:
time: 149 us; the launch traced here: 147 us
  Pallas kernels  146 us (98%)
    pallas_call x1, Pallas kernels, local(): pl.pallas_call(kernel, name='expert_layer', out_shape=(piece, piece, grad...  143 us

profile of v5, /device:TPU:34, one launch (start us, length us, event | category | flops | bytes accessed | tf_op | source)
XLA Modules:
  0.0 146.5 jit_solution(5365097339225760970)
XLA Ops:
  0.6 142.8 %expert_layer.1 = (bf16[2,256,896]{2,1,0:T(8,128)(2,1)}, bf16[2,256,896]{2,1,0:T(8,128)(2,1)}, f32[448,256]{1,0:T(8,128)}, f32[448,256]{1,0:T(8,128)}, f32[448,256]{1,0:T(8,128)}) custom-call(bf16[2,256,7168]{2,1,0:T(8,128)(2,1)} %acts.1, s32[1,2]{1,0:T(1,128)} %counts.1, bf16[448,256]{1,0:T(8,128)(2,1)} %gate_w.1, bf16[448,256]{1,0:T(8,128)(2,1)} %up_w.1, ...), custom_call_target="tpu_custom_call" | custom-call | tf_op jit(solution)/shard_map/expert_layer/pallas_call | solution.py:578
  143.4 2.9 %hand_on.1 = (bf16[2,256,896]{2,1,0:T(8,128)(2,1)}, bf16[2,256,896]{2,1,0:T(8,128)(2,1)}, f32[448,256]{1,0:T(8,128)}, f32[448,256]{1,0:T(8,128)}, f32[448,256]{1,0:T(8,128)}) custom-call(bf16[2,256,896]{2,1,0:T(8,128)(2,1)} %get-tuple-element.10.refs_0_, bf16[2,256,896]{2,1,0:T(8,128)(2,1)} %get-tuple-element.11.refs_1_, ...), custom_call_target="tpu_custom_call" | custom-call | tf_op jit(solution)/shard_map/hand_on/pallas_call | solution.py:616

commit v6 on v5

--- a/solution.py
+++ b/solution.py
@@ -529,15 +529,15 @@
     columns_done(GATE)
     columns_product(GGP, GATE, store_first)
     columns.append(quarters_in())
+    columns_done(DOWN)
+    columns_product(HIDDEN, DOWN, store_mixed)
+    write_out(mixed, 0)
     gather_done(GUP)
     columns_done(UP)
     columns_product(GUP, UP, store_second)
     write_out(input_grad, 1)
     x_sums(UP)
     z_sums(GATE)
-    columns_done(DOWN)
-    columns_product(HIDDEN, DOWN, store_mixed)
-    write_out(mixed, 0)
     z_sums(UP)
     finish_weight_sends(UP)
     finish_weight_sends(DOWN)

time: 149 us -> 155 us (1.040)
  the two profiles are of different devices: /device:TPU:34 before, /device:TPU:11 now
where the time goes in v6:
time: 155 us
  Pallas kernels  154 us (99%)
    pallas_call x1, Pallas kernels, local(): pl.pallas_call(kernel, name='expert_layer', out_shape=(piece, piece, grad...  151 us

profile of v6, /device:TPU:11, one launch (start us, length us, event | category | flops | bytes accessed | tf_op | source)
XLA Modules:
  0.0 154.9 jit_solution(1043654606931090781)
XLA Ops:
  0.6 151.2 %expert_layer.1 = (bf16[2,256,896]{2,1,0:T(8,128)(2,1)}, bf16[2,256,896]{2,1,0:T(8,128)(2,1)}, f32[448,256]{1,0:T(8,128)}, f32[448,256]{1,0:T(8,128)}, f32[448,256]{1,0:T(8,128)}) custom-call(bf16[2,256,7168]{2,1,0:T(8,128)(2,1)} %acts.1, s32[1,2]{1,0:T(1,128)} %counts.1, bf16[448,256]{1,0:T(8,128)(2,1)} %gate_w.1, bf16[448,256]{1,0:T(8,128)(2,1)} %up_w.1, ...), custom_call_target="tpu_custom_call" | custom-call | tf_op jit(solution)/shard_map/expert_layer/pallas_call | solution.py:578
  151.8 2.9 %hand_on.1 = (bf16[2,256,896]{2,1,0:T(8,128)(2,1)}, bf16[2,256,896]{2,1,0:T(8,128)(2,1)}, f32[448,256]{1,0:T(8,128)}, f32[448,256]{1,0:T(8,128)}, f32[448,256]{1,0:T(8,128)}) custom-call(bf16[2,256,896]{2,1,0:T(8,128)(2,1)} %get-tuple-element.10.refs_0_, bf16[2,256,896]{2,1,0:T(8,128)(2,1)} %get-tuple-element.11.refs_1_, ...), custom_call_target="tpu_custom_call" | custom-call | tf_op jit(solution)/shard_map/hand_on/pallas_call | solution.py:616

commit v7 on v5

--- a/solution.py
+++ b/solution.py
@@ -234,7 +234,7 @@
     TILE = 64
 
     gathers = []
-    MIDDLE, TOP = ROWS // 2, 256
+    MIDDLE, TOP = ROWS // 2, 224
     LOW = (ROWS - TOP) // 2
 
     def act_ref(a, flip, k, low=0, size=ROWS):

time: 149 us -> 150 us (level)
  no operation moved by 1% of the time
where the time goes in v7:
time: 150 us; the launch traced here: 148 us
  Pallas kernels  147 us (98%)
    pallas_call x1, Pallas kernels, local(): pl.pallas_call(kernel, name='expert_layer', out_shape=(piece, piece, grad...  144 us

profile of v7, /device:TPU:34, one launch (start us, length us, event | category | flops | bytes accessed | tf_op | source)
XLA Modules:
  0.0 147.9 jit_solution(16881036085555768393)
XLA Ops:
  0.6 144.2 %expert_layer.1 = (bf16[2,256,896]{2,1,0:T(8,128)(2,1)}, bf16[2,256,896]{2,1,0:T(8,128)(2,1)}, f32[448,256]{1,0:T(8,128)}, f32[448,256]{1,0:T(8,128)}, f32[448,256]{1,0:T(8,128)}) custom-call(bf16[2,256,7168]{2,1,0:T(8,128)(2,1)} %acts.1, s32[1,2]{1,0:T(1,128)} %counts.1, bf16[448,256]{1,0:T(8,128)(2,1)} %gate_w.1, bf16[448,256]{1,0:T(8,128)(2,1)} %up_w.1, ...), custom_call_target="tpu_custom_call" | custom-call | tf_op jit(solution)/shard_map/expert_layer/pallas_call | solution.py:578
  144.8 2.9 %hand_on.1 = (bf16[2,256,896]{2,1,0:T(8,128)(2,1)}, bf16[2,256,896]{2,1,0:T(8,128)(2,1)}, f32[448,256]{1,0:T(8,128)}, f32[448,256]{1,0:T(8,128)}, f32[448,256]{1,0:T(8,128)}) custom-call(bf16[2,256,896]{2,1,0:T(8,128)(2,1)} %get-tuple-element.10.refs_0_, bf16[2,256,896]{2,1,0:T(8,128)(2,1)} %get-tuple-element.11.refs_1_, ...), custom_call_target="tpu_custom_call" | custom-call | tf_op jit(solution)/shard_map/hand_on/pallas_call | solution.py:616
